TPU v7x, 32 devices: a whole 2x2x4 slice. The times are simulated.
32 devices in a mesh: groups: 2 (over x), expert: 16 (over z, y, core).
Axes of the slice: x: 2, y: 2, z: 4, core: 2. Of those that a mesh axis runs over, the one named last changes fastest.
Arguments:
- cotangent: bfloat16 [4096, 4096], P(('groups', 'expert')), parts along dimension 0, may hold values from -6 to 6
- expert_ids: int32 [4096, 8], P(('groups', 'expert')), parts along dimension 0, may hold values from 0 to 15, all different within a row; in each aligned block of 128 rows (0 to 127, 128 to 255, ...) at most 80 rows name the same one
- gate_probs: bfloat16 [4096, 8], P(('groups', 'expert')), parts along dimension 0, may hold values from 0.019897461 to 0.5
- seq_ids: int32 [4096], P(('groups', 'expert')), parts along dimension 0, may hold values from 0 to 1, never falling along the last dimension, each value on 1 to 2047 neighbouring positions
- hidden_saved: bfloat16 [32, 1280, 768], P(('groups', 'expert')), parts along dimension 0, may hold values from -2 to 2
Outputs:
- fisher: bfloat16 [32, 768, 4096], P(('groups', 'expert')), parts along dimension 0
There are 2 independent parts, one for each index of `groups`. A program takes and returns all parts, laid end to end along the dimension named above; each array names one. Nothing has to cross between parts.
Inputs may be any that keep to these rules, and one draw needn't show every extreme that they name: `expert_ids`: each row names 8 different experts; among the 128 tokens of one device no expert is named more than 80 times, and this bound is reached. `seq_ids`: never falling along the tokens; each sequence has 1 to 2047 tokens.
All inputs are finite; a program needn't handle non-finite values.
Results may differ from a plain program's by a relative error of at most 0.0052.
Values may be sent and summed in bfloat16 or wider, within the bound.
A program may use at most 128 MiB of HBM per device.

v0:
```python
import jax
import jax.numpy as jnp
from jax import lax
from jax.sharding import PartitionSpec as P

SEQ_AVG = 8192


def fisher_columns(arrived, hidden_rows, seq_table, seq_count, window):
    owners, cap_rows = seq_table.shape
    flat_rows = arrived.reshape(owners * cap_rows, arrived.shape[-1])
    flat_seq = seq_table.reshape(-1)
    block_last = lax.cummax(jnp.max(seq_table, axis=1), axis=0)
    span = window * cap_rows

    def one_sequence(sequence, totals):
        first_block = jnp.sum((block_last < sequence).astype(jnp.int32))
        offset = first_block * cap_rows
        hidden_part = lax.dynamic_slice_in_dim(hidden_rows, offset, span, 0)
        row_part = lax.dynamic_slice_in_dim(flat_rows, offset, span, 0)
        seq_part = lax.dynamic_slice_in_dim(flat_seq, offset, span, 0)
        chosen = jnp.where(
            (seq_part == sequence)[:, None], hidden_part, jnp.zeros_like(hidden_part)
        )
        grad_part = lax.dot_general(
            chosen, row_part, (((0,), (0,)), ((), ())), preferred_element_type=jnp.float32
        )
        return totals + grad_part * grad_part

    empty = jnp.zeros((hidden_rows.shape[1], arrived.shape[-1]), jnp.float32)
    totals = lax.fori_loop(0, seq_count, one_sequence, empty)
    return totals.astype(jnp.bfloat16)


def shards(cotangent, expert_ids, gate_probs, seq_ids, hidden_saved):
    owners = lax.axis_size("expert")
    tok_dev = expert_ids.shape[0]
    cap_rows = hidden_saved.shape[1] // owners
    total_tokens = tok_dev * owners
    seq_count = total_tokens // SEQ_AVG + 2
    seq_longest = min(SEQ_AVG * 9 // 8, total_tokens - seq_count + 1)
    window = min(seq_longest // tok_dev + 2, owners)
    expert_iota = jnp.arange(owners, dtype=jnp.int32)
    per_expert = jnp.sum(
        (expert_ids[:, :, None] == expert_iota[None, None, :]).astype(jnp.int32), axis=1
    )
    arrival = jnp.cumsum(per_expert, axis=0) - per_expert
    pair_rank = jnp.take_along_axis(arrival, expert_ids, axis=1)
    pair_slot = expert_ids * cap_rows + pair_rank
    slot_iota = jnp.arange(owners * cap_rows, dtype=jnp.int32)
    placed = slot_iota[:, None, None] == pair_slot[None, :, :]
    weights = jnp.where(placed, gate_probs.astype(jnp.float32)[None, :, :], 0.0)
    dispatch = jnp.sum(weights, axis=2).astype(jnp.bfloat16)
    outgoing = jnp.dot(dispatch, cotangent, preferred_element_type=jnp.float32).astype(jnp.bfloat16)
    outgoing = outgoing.reshape(owners, cap_rows, cotangent.shape[1])
    seq_spread = jnp.broadcast_to(seq_ids[:, None], expert_ids.shape)
    outgoing_seq = (
        jnp.full((owners, cap_rows), -1, jnp.int32).at[expert_ids, pair_rank].set(seq_spread)
    )
    seq_table = lax.all_to_all(outgoing_seq, "expert", split_axis=0, concat_axis=0, tiled=True)
    hidden_rows = hidden_saved[0]
    fisher = fisher_columns(
        lax.all_to_all(outgoing, "expert", split_axis=0, concat_axis=0, tiled=True),
        hidden_rows,
        seq_table,
        seq_count,
        window,
    )
    return fisher[None]


def solution(mesh):
    return jax.shard_map(
        shards,
        mesh=mesh,
        in_specs=(
            P(("groups", "expert"), None),
            P(("groups", "expert"), None),
            P(("groups", "expert"), None),
            P(("groups", "expert")),
            P(("groups", "expert"), None, None),
        ),
        out_specs=P(("groups", "expert"), None, None),
        check_vma=False,
    )
```

profile of v0, /device:TPU:15, one launch (start us, length us, event | category | flops | bytes accessed | tf_op | source)
XLA Modules:
  0.0 308.2 jit_solution(17333613380428913132)
XLA Ops:
  0.0 0.8 shift-left_or_fusion
  0.8 0.7 convert_reduce_fusion
  1.5 0.1 copy.54
  1.6 0.1 copy.56
  1.7 0.1 reshape.48
  1.8 0.2 reduce_window_sum.11
  2.0 0.0 copy-start.2
  2.0 0.0 copy-start.6
  2.0 0.0 copy-start.5
  2.0 0.0 copy-start.3
  2.0 7.1 %gather_fusion = s32[1024]{0:T(1024)S(1)} fusion(s32[128,16]{1,0:T(8,128)S(1)} %sub.3, s32[1024]{0:T(1024)S(1)} %reshape.48), kind=kCustom, calls=%fused_computation | custom fusion | bytes 16384 | tf_op jit(solution)/shard_map/jit(take_along_axis)/gather | solution.py:48
  9.1 0.1 reshape.51
  9.3 0.1 and_reduce_fusion
  9.4 0.1 multiply_reduce_fusion
  9.4 0.1 copy.58
  9.5 0.1 reshape.54
  9.7 0.1 broadcast_in_dim.65
  9.7 0.1 reshape.56
  9.8 4.3 %scatter_custom_fusion = s32[1280]{0:T(1024)S(1)} fusion(s32[1024]{0:T(1024)S(1)} %reshape.54, s32[1024]{0:T(1024)S(1)} %reshape.56, s32[]{:T(128)} %constant.56.clone.1), kind=kCustom, calls=%fused_computation.22 | custom fusion | bytes 5124
  14.2 0.7 all_to_all.9
  14.8 6.6 %all-to-all-start = ((s32[16,1,80]{2,1,0:T(1,128)}), s32[16,1,80]{2,1,0:T(1,128)S(1)}, u32[]{:S(2)}, u32[]{:S(2)}) async-start(s32[16,1,80]{2,1,0:T(1,128)} %all_to_all.9), calls=%async_computation | async-start | bytes 16384 | tf_op jit(solution)/shard_map/all_to_all | solution.py:60
  21.4 6.8 %select_reduce_fusion = bf16[1280,128]{1,0:T(8,128)(2,1)S(1)} fusion(f32[128,8]{0,1:T(8,128)S(1)} %convert_element_type.19, s32[128,8]{0,1:T(8,128)S(1)} %get-tuple-element.139), kind=kLoop, calls=%fused_computation.10 | loop fusion | flops 3768320 | bytes 335872 | tf_op jit(solution)/shard_map/reduce_sum | solution.py:53
  28.2 5.4 %convolution_convert_fusion = bf16[1280,4096]{1,0:T(8,128)(2,1)} fusion(bf16[128,4096]{1,0:T(8,128)(2,1)S(1)} %copy-done, bf16[1280,128]{1,0:T(8,128)(2,1)S(1)} %select_reduce_fusion), kind=kOutput, calls=%fused_computation.8 | convolution fusion | flops 1347420160 | bytes 11862016 | tf_op jit(solution)/shard_map/dot_general | solution.py:54
  33.6 6.2 %all-to-all-start.1 = ((bf16[16,80,4096]{2,1,0:T(8,128)(2,1)}), bf16[16,80,4096]{2,1,0:T(8,128)(2,1)}, u32[]{:S(2)}, u32[]{:S(2)}) async-start(bf16[16,80,4096]{2,1,0:T(8,128)(2,1)} %bitcast.20), calls=%async_computation.1 | async-start | bytes 20971520 | tf_op jit(solution)/shard_map/all_to_all | solution.py:63
  39.7 0.6 broadcast.85
  40.3 0.7 reduce.8
  41.0 0.1 reshape.40
  41.1 225.9 %all-to-all-done.1 = bf16[16,80,4096]{2,1,0:T(8,128)(2,1)} async-done(((bf16[16,80,4096]{2,1,0:T(8,128)(2,1)}), bf16[16,80,4096]{2,1,0:T(8,128)(2,1)}, u32[]{:S(2)}, u32[]{:S(2)}) %all-to-all-start.1) | async-done | bytes 10485792 | tf_op jit(solution)/shard_map/all_to_all | solution.py:63
  267.0 32.9 %while.14 = (s32[]{:T(128)}, f32[768,4096]{1,0:T(8,128)}, s32[1280]{0:T(1024)S(1)}, bf16[1280,768]{1,0:T(8,128)(2,1)S(1)}, bf16[1280,4096]{1,0:T(8,128)(2,1)}, /*index=5*/s32[]{:T(128)}, s32[]{:T(128)}) while((s32[]{:T(128)}, f32[768,4096]{1,0:T(8,128)}, s32[1280]{0:T(1024)S(1)}, bf16[1280,768]{1,0:T(8,128)(2,1)S(1)}, ...), condition=%wide.region_5.6_spmd.clone, body=%wide.region_4.5_spmd.clone.sunk | while | flops 8063485440 | bytes 37625440 | solution.py:31
  267.0 15.6 %select_add_fusion.2 = f32[768,4096]{1,0:T(8,128)} fusion(f32[768,4096]{1,0:T(8,128)} %get-tuple-element.181, bf16[1280,4096]{1,0:T(8,128)(2,1)} %get-tuple-element.191, pred[]{:T(512)S(6)} %compare.7, bf16[1280,768]{1,0:T(8,128)(2,1)S(1)} %get-tuple-element.190, pred[1280]{0:T(1024)(128)(4,1)S(1)} %broadcast_compare_fusion.2), kind=kOutput, calls=%fused_computation.2.clone.1 | convolution fusion | flops 8063483904 | bytes 37618944 | tf_op jit(solution)/shard_map/while/body/eval_jaxpr/dot_general | solution.py:25
  282.6 17.3 %select_add_fusion.2 = f32[768,4096]{1,0:T(8,128)} fusion(f32[768,4096]{1,0:T(8,128)} %get-tuple-element.181, bf16[1280,4096]{1,0:T(8,128)(2,1)} %get-tuple-element.191, pred[]{:T(512)S(6)} %compare.7, bf16[1280,768]{1,0:T(8,128)(2,1)S(1)} %get-tuple-element.190, pred[1280]{0:T(1024)(128)(4,1)S(1)} %broadcast_compare_fusion.2), kind=kOutput, calls=%fused_computation.2.clone.1 | convolution fusion | flops 8063483904 | bytes 37618944 | tf_op jit(solution)/shard_map/while/body/eval_jaxpr/dot_general | solution.py:25
  299.9 8.2 %convert_bitcast_fusion = bf16[1,768,4096]{2,1,0:T(8,128)(2,1)} fusion(f32[768,4096]{1,0:T(8,128)} %get-tuple-element.110), kind=kLoop, calls=%fused_computation.9 | loop fusion | flops 3145728 | bytes 18874368 | tf_op jit(solution)/shard_map/broadcast_in_dim | solution.py:69
  (19 shorter events, 0.1 us)
Async XLA Ops:
  0.0 28.2 %copy-start = (bf16[128,4096]{1,0:T(8,128)(2,1)S(1)}, bf16[128,4096]{1,0:T(8,128)(2,1)}, u32[]{:S(2)}) copy-start(bf16[128,4096]{1,0:T(8,128)(2,1)} %param.7) | copy-start | bytes 3145732
  2.0 7.3 %copy-start.2 = (s32[128,8]{0,1:T(8,128)S(1)}, s32[128,8]{0,1:T(8,128)}, u32[]{:S(2)}) copy-start(s32[128,8]{0,1:T(8,128)} %param.8) | copy-start | bytes 12292
  2.0 7.3 %copy-start.6 = (s32[2]{0:T(128)S(1)}, s32[2]{0:T(128)}, u32[]{:S(2)}) copy-start(s32[2]{0:T(128)} %constant.61) | copy-start | bytes 28
  2.0 7.4 %copy-start.5 = (s32[2]{0:T(128)S(1)}, s32[2]{0:T(128)}, u32[]{:S(2)}) copy-start(s32[2]{0:T(128)} %constant.58) | copy-start | bytes 28
  2.0 7.6 %copy-start.4 = (s32[128]{0:T(128)S(1)}, s32[128]{0:T(128)}, u32[]{:S(2)}) copy-start(s32[128]{0:T(128)} %param.10) | copy-start | bytes 1540
  2.0 19.4 %copy-start.3 = (bf16[128,8]{0,1:T(8,128)(2,1)S(1)}, bf16[128,8]{0,1:T(8,128)(2,1)}, u32[]{:S(2)}) copy-start(bf16[128,8]{0,1:T(8,128)(2,1)} %param.9) | copy-start | bytes 6148
  14.8 18.7 %all-to-all-start = ((s32[16,1,80]{2,1,0:T(1,128)}), s32[16,1,80]{2,1,0:T(1,128)S(1)}, u32[]{:S(2)}, u32[]{:S(2)}) async-start(s32[16,1,80]{2,1,0:T(1,128)} %all_to_all.9), calls=%async_computation | async-start | bytes 16384 | tf_op jit(solution)/shard_map/all_to_all | solution.py:60
  33.6 233.4 %copy-start.1 = (bf16[1,1280,768]{2,1,0:T(8,128)(2,1)S(1)}, bf16[1,1280,768]{2,1,0:T(8,128)(2,1)}, u32[]{:S(2)}) copy-start(bf16[1,1280,768]{2,1,0:T(8,128)(2,1)} %param.11) | copy-start | bytes 5898244
  33.6 233.4 %all-to-all-start.1 = ((bf16[16,80,4096]{2,1,0:T(8,128)(2,1)}), bf16[16,80,4096]{2,1,0:T(8,128)(2,1)}, u32[]{:S(2)}, u32[]{:S(2)}) async-start(bf16[16,80,4096]{2,1,0:T(8,128)(2,1)} %bitcast.20), calls=%async_computation.1 | async-start | bytes 20971520 | tf_op jit(solution)/shard_map/all_to_all | solution.py:63
where the time goes:
time: 309 us; the launch traced here: 308 us
  waiting for transfers between devices  226 us (73%)
  matrix products  38.3 us (12%)
  other arithmetic  17.6 us (6%)
  local copies, waits for them, and re-layouts  13.5 us (4%)
  starting transfers between devices  12.7 us (4%)
    all_to_all x1, waiting for transfers between devices, shards(): lax.all_to_all(outgoing, 'expert', split_axis=0, concat_axis=0, tiled=True)  226 us
    dot_general x2, matrix products, one_sequence(): lax.dot_general(chosen, row_part, (((0,), (0,)), ((), ())), preferred_ele...  32.9 us
    broadcast_in_dim x1, other arithmetic, shards(): return fisher[None]  8.24 us
    gather x5, local copies, waits for them, and re-layouts, shards(): pair_rank = jnp.take_along_axis(arrival, expert_ids, axis=1)  7.39 us
    reduce_sum x1, other arithmetic, shards(): dispatch = jnp.sum(weights, axis=2).astype(jnp.bfloat16)  6.78 us
    all_to_all x1, starting transfers between devices, shards(): lax.all_to_all(outgoing_seq, 'expert', split_axis=0, concat_axis=0, tiled...  6.55 us
  transfers between devices with their start and end apart: 2, of which 1 were waited for; matrix products, arithmetic and copies ran while one was open for 4% of the time, Pallas kernels for 0%

commit v1 on v0

--- a/solution.py
+++ b/solution.py
@@ -1,9 +1,14 @@
+import functools
+
 import jax
 import jax.numpy as jnp
 from jax import lax
+from jax.experimental import pallas as pl
+from jax.experimental.pallas import tpu as pltpu
 from jax.sharding import PartitionSpec as P
 
 SEQ_AVG = 8192
+CHUNKS = 8
 
 
 def fisher_columns(arrived, hidden_rows, seq_table, seq_count, window):
@@ -69,9 +74,302 @@
     return fisher[None]
 
 
+MESH = pl.DeviceIdType.MESH
+UP, DOWN, ACROSS, SIBLING = range(4)
+
+
+def gather_kernel(
+    layers, cap_rows, seq_count, chunks,
+    cot_ref, meta_ref, hidden_ref, out_ref,
+    rows_all, meta_all, hidden_buf, hidden_t, pick_w, slot_rows, stage,
+    own_sem, hidden_sem, out_sem, send_sem, recv_sem, meta_send, meta_recv,
+):
+    places = 2 * layers
+    tok_dev, width = rows_all.shape[3:]
+    ffw = hidden_t.shape[0]
+    me = lax.axis_index("expert")
+    core = lax.rem(me, 2)
+    place = me // 2
+    y = lax.rem(place, 2)
+    z = place // 2
+    has_up, has_down = z < layers - 1, z > 0
+    device = {UP: me + 4, DOWN: me - 4, ACROSS: me + 2 - 4 * y, SIBLING: me + 1 - 2 * core}
+
+    def own_copy(c):
+        columns = pl.ds(pl.multiple_of(c * width, width), width)
+        return pltpu.make_async_copy(cot_ref.at[:, columns], rows_all.at[c, core, place], own_sem.at[c])
+
+    def rows_copy(c, plane, origin, way):
+        return pltpu.make_async_remote_copy(
+            src_ref=rows_all.at[c, plane, origin],
+            dst_ref=rows_all.at[c, plane, origin],
+            send_sem=send_sem.at[c, origin, way],
+            recv_sem=recv_sem.at[c, plane, origin],
+            device_id={"expert": device[way]},
+            device_id_type=MESH,
+        )
+
+    def meta_copy(plane, origin, way):
+        return pltpu.make_async_remote_copy(
+            src_ref=meta_all.at[plane, origin],
+            dst_ref=meta_all.at[plane, origin],
+            send_sem=meta_send.at[origin, way],
+            recv_sem=meta_recv.at[plane, origin],
+            device_id={"expert": device[way]},
+            device_id_type=MESH,
+        )
+
+    def out_copy(c):
+        columns = pl.ds(pl.multiple_of(c * width, width), width)
+        slot = lax.rem(c, 2)
+        return pltpu.make_async_copy(stage.at[slot], out_ref.at[0, :, columns], out_sem.at[slot])
+
+    def send(c, origin, ways):
+        @pl.when(c == 0)
+        def _():
+            for way in ways:
+                meta_copy(core, origin, way).start()
+
+        for way in ways:
+            rows_copy(c, core, origin, way).start()
+
+    def arrive(c, plane, origin):
+        @pl.when(c == 0)
+        def _():
+            meta_copy(plane, origin, SIBLING).wait_recv()
+
+        rows_copy(c, plane, origin, SIBLING).wait_recv()
+
+    hidden_copy = pltpu.make_async_copy(hidden_ref.at[0], hidden_buf, hidden_sem)
+    for c in range(chunks):
+        own_copy(c).start()
+    hidden_copy.start()
+    meta_all[core, place] = meta_ref[...]
+
+    barrier = pltpu.get_barrier_semaphore()
+    for way in (ACROSS, SIBLING):
+        pl.semaphore_signal(barrier, inc=1, device_id={"expert": device[way]}, device_id_type=MESH)
+    for way, there in ((UP, has_up), (DOWN, has_down)):
+        @pl.when(there)
+        def _():
+            pl.semaphore_signal(barrier, inc=1, device_id={"expert": device[way]}, device_id_type=MESH)
+    pl.semaphore_wait(barrier, 2 + has_up.astype(jnp.int32) + has_down.astype(jnp.int32))
+
+    def start_own(c):
+        own_copy(c).wait()
+
+        @pl.when(has_up)
+        def _():
+            send(c, place, (UP,))
+
+        @pl.when(has_down)
+        def _():
+            send(c, place, (DOWN,))
+
+        send(c, place, (ACROSS, SIBLING))
+
+    def relay(c, hop):
+        for source, there, onward, way in (
+            (z - hop, z >= hop, has_up, UP),
+            (z + hop, z + hop < layers, has_down, DOWN),
+        ):
+            @pl.when(there)
+            def _():
+                origin = source * 2 + y
+                arrive(c, core, origin)
+
+                @pl.when(onward)
+                def _():
+                    send(c, origin, (way,))
+
+                send(c, origin, (ACROSS, SIBLING))
+
+    def from_across(c):
+        for layer in range(layers):
+            origin = layer * 2 + 1 - y
+            arrive(c, core, origin)
+            send(c, origin, (SIBLING,))
+
+    def transpose_hidden():
+        hidden_copy.wait()
+
+        def one(i, _):
+            rows = pl.ds(pl.multiple_of(i * 128, 128), 128)
+            hidden_t[:, rows] = hidden_buf[rows, :].T
+            return 0
+
+        lax.fori_loop(0, hidden_buf.shape[0] // 128, one, 0)
+
+    def prepare():
+        earlier = lax.broadcasted_iota(jnp.int32, (tok_dev, tok_dev), 0) < lax.broadcasted_iota(
+            jnp.int32, (tok_dev, tok_dev), 1
+        )
+        earlier = earlier.astype(jnp.float32).astype(jnp.bfloat16)
+        slots = lax.broadcasted_iota(jnp.int32, (cap_rows, tok_dev), 0).astype(jnp.float32)
+        expert = me.astype(jnp.float32)
+        top = meta_all.shape[2] // 3
+        for plane in range(2):
+            table = meta_all[plane]
+            named = table[:, :top, :] == expert
+            routed = jnp.sum(jnp.where(named, 1.0, 0.0), axis=1)
+            gate = jnp.sum(jnp.where(named, table[:, top:2 * top, :], 0.0), axis=1)
+            rank = jnp.dot(routed.astype(jnp.bfloat16), earlier, preferred_element_type=jnp.float32)
+            for origin in range(places):
+                here = routed[origin:origin + 1] > 0
+                sequence = table[origin, 2 * top:2 * top + 1, :]
+                for s in range(seq_count):
+                    spot = jnp.where(here & (sequence == float(s)), rank[origin:origin + 1], -1.0)
+                    weight = jnp.where(slots == spot, gate[origin:origin + 1], 0.0)
+                    pick_w[plane, origin, s * cap_rows:(s + 1) * cap_rows, :] = weight.astype(jnp.bfloat16)
+
+    def finish(c):
+        for origin in range(places):
+            arrive(c, 1 - core, origin)
+
+        @pl.when(c == 0)
+        def _():
+            prepare()
+
+        def dispatch(origin, _):
+            for plane in range(2):
+                sent = jnp.dot(
+                    pick_w[plane, origin], rows_all[c, plane, origin], preferred_element_type=jnp.float32
+                ).astype(jnp.bfloat16)
+                first = pl.multiple_of((origin * 2 + plane) * cap_rows, 16)
+                for s in range(seq_count):
+                    slot_rows[s, pl.ds(first, cap_rows), :] = sent[s * cap_rows:(s + 1) * cap_rows]
+            return 0
+
+        lax.fori_loop(0, places, dispatch, 0)
+
+        @pl.when(c >= 2)
+        def _():
+            out_copy(c - 2).wait()
+
+        slot = lax.rem(c, 2)
+        tall = 256
+
+        def squares(m, _):
+            part = pl.ds(pl.multiple_of(m * tall, tall), tall)
+            total = None
+            for s in range(seq_count):
+                grad = jnp.dot(hidden_t[part, :], slot_rows[s], preferred_element_type=jnp.float32)
+                total = grad * grad if total is None else total + grad * grad
+            stage[slot, part, :] = total.astype(jnp.bfloat16)
+            return 0
+
+        lax.fori_loop(0, ffw // tall, squares, 0)
+        out_copy(c).start()
+
+    def within(c, act):
+        @pl.when((c >= 0) & (c < chunks))
+        def _():
+            act(c)
+
+    def step(t, _):
+        within(t, start_own)
+
+        @pl.when(t == 1)
+        def _():
+            transpose_hidden()
+
+        for hop in range(layers - 1, 0, -1):
+            within(t - hop, lambda c: relay(c, hop))
+        within(t - layers, from_across)
+        within(t - layers - 1, finish)
+        return 0
+
+    lax.fori_loop(0, chunks + layers + 1, step, 0)
+
+    def sent_all(c, wait):
+        for layer in range(layers):
+            @pl.when(has_up & (layer <= z))
+            def _():
+                wait(layer * 2 + y, UP)
+
+            @pl.when(has_down & (layer >= z))
+            def _():
+                wait(layer * 2 + y, DOWN)
+
+            wait(layer * 2 + y, ACROSS)
+            wait(layer * 2 + y, SIBLING)
+            wait(layer * 2 + 1 - y, SIBLING)
+
+    def drain(c, _):
+        sent_all(c, lambda origin, way: rows_copy(c, core, origin, way).wait_send())
+        return 0
+
+    lax.fori_loop(0, chunks, drain, 0)
+    sent_all(0, lambda origin, way: meta_copy(core, origin, way).wait_send())
+    for c in range(max(chunks - 2, 0), chunks):
+        out_copy(c).wait()
+
+
+def gather_shards(cotangent, expert_ids, gate_probs, seq_ids, hidden_saved):
+    owners = lax.axis_size("expert")
+    tok_dev, depth = cotangent.shape
+    slots, ffw = hidden_saved.shape[1:]
+    cap_rows = slots // owners
+    seq_count = tok_dev * owners // SEQ_AVG + 2
+    layers = owners // 4
+    chunks = CHUNKS
+    width = depth // chunks
+    top = expert_ids.shape[1]
+    meta = jnp.concatenate(
+        [
+            expert_ids.T.astype(jnp.float32),
+            gate_probs.T.astype(jnp.float32),
+            jnp.broadcast_to(seq_ids.astype(jnp.float32)[None, :], (top, tok_dev)),
+        ],
+        axis=0,
+    )
+    return pl.pallas_call(
+        functools.partial(gather_kernel, layers, cap_rows, seq_count, chunks),
+        out_shape=jax.ShapeDtypeStruct((1, ffw, depth), jnp.bfloat16),
+        in_specs=[
+            pl.BlockSpec(memory_space=pl.ANY),
+            pl.BlockSpec(memory_space=pltpu.VMEM),
+            pl.BlockSpec(memory_space=pl.ANY),
+        ],
+        out_specs=pl.BlockSpec(memory_space=pl.ANY),
+        scratch_shapes=[
+            pltpu.VMEM((chunks, 2, 2 * layers, tok_dev, width), jnp.bfloat16),
+            pltpu.VMEM((2, 2 * layers, 3 * top, tok_dev), jnp.float32),
+            pltpu.VMEM((slots, ffw), jnp.bfloat16),
+            pltpu.VMEM((ffw, slots), jnp.bfloat16),
+            pltpu.VMEM((2, 2 * layers, seq_count * cap_rows, tok_dev), jnp.bfloat16),
+            pltpu.VMEM((seq_count, slots, width), jnp.bfloat16),
+            pltpu.VMEM((2, ffw, width), jnp.bfloat16),
+            pltpu.SemaphoreType.DMA((chunks,)),
+            pltpu.SemaphoreType.DMA,
+            pltpu.SemaphoreType.DMA((2,)),
+            pltpu.SemaphoreType.DMA((chunks, 2 * layers, 4)),
+            pltpu.SemaphoreType.DMA((chunks, 2, 2 * layers)),
+            pltpu.SemaphoreType.DMA((2 * layers, 4)),
+            pltpu.SemaphoreType.DMA((2, 2 * layers)),
+        ],
+        cost_estimate=pl.CostEstimate(
+            flops=2 * seq_count * slots * ffw * depth,
+            bytes_accessed=2 * depth * (ffw + tok_dev) + 2 * slots * ffw,
+            transcendentals=0,
+        ),
+        compiler_params=pltpu.CompilerParams(
+            collective_id=0, has_side_effects=True, vmem_limit_bytes=52 * 1024 * 1024
+        ),
+    )(cotangent, meta, hidden_saved)
+
+
+def parts(cotangent, expert_ids, gate_probs, seq_ids, hidden_saved):
+    owners = lax.axis_size("expert")
+    cap_rows = hidden_saved.shape[1] // owners
+    gathers = owners == 16 and cap_rows % 16 == 0 and 2 * cap_rows > expert_ids.shape[0]
+    plan = gather_shards if gathers else shards
+    return plan(cotangent, expert_ids, gate_probs, seq_ids, hidden_saved)
+
+
 def solution(mesh):
     return jax.shard_map(
-        shards,
+        parts,
         mesh=mesh,
         in_specs=(
             P(("groups", "expert"), None),

time: 309 us -> 120 us (0.39)
  the two profiles are of different devices: /device:TPU:15 before, /device:TPU:0 now
where the time goes in v1:
time: 120 us
  Pallas kernels  111 us (92%)
  local copies, waits for them, and re-layouts  7.51 us (6%)
  other arithmetic  2.03 us (2%)
    pallas_call x1, Pallas kernels, gather_shards(): pl.pallas_call(functools.partial(gather_kernel, layers, cap_rows, seq_cou...  111 us
    unnamed x3, local copies, waits for them, and re-layouts  7.51 us

profile of v1, /device:TPU:0, one launch (start us, length us, event | category | flops | bytes accessed | tf_op | source)
XLA Modules:
  0.0 120.2 jit_solution(14457626532856944929)
XLA Ops:
  0.0 0.7 convert_element_type.19
  0.7 0.7 convert_bitcast_fusion.1
  1.4 0.7 convert_bitcast_fusion
  2.0 0.0 copy-start
  2.0 1.2 %copy-done = bf16[128,4096]{1,0:T(8,128)(2,1)S(1)} copy-done((bf16[128,4096]{1,0:T(8,128)(2,1)S(1)}, bf16[128,4096]{1,0:T(8,128)(2,1)}, u32[]{:S(2)}) %copy-start) | copy-done | bytes 1048600
  3.3 110.7 %shard_map.55 = bf16[1,768,4096]{2,1,0:T(8,128)(2,1)} custom-call(bf16[128,4096]{1,0:T(8,128)(2,1)S(1)} %copy-done, f32[24,128]{1,0:T(8,128)S(1)} %pad_maximum_fusion.meta_ref, bf16[1,1280,768]{2,1,0:T(8,128)(2,1)} %hidden_ref.1), custom_call_target="tpu_custom_call" | custom-call | flops 16106127360 | bytes 9306112 | tf_op jit(solution)/shard_map/pallas_call | solution.py:326
  114.0 6.3 %copy.7 = bf16[1,768,4096]{2,1,0:T(8,128)(2,1)} copy(bf16[1,768,4096]{2,1,0:T(8,128)(2,1)} %shard_map.55) | data formatting | bytes 12582912
  (2 shorter events, 0.0 us)
Async XLA Ops:
  2.0 1.2 %copy-start = (bf16[128,4096]{1,0:T(8,128)(2,1)S(1)}, bf16[128,4096]{1,0:T(8,128)(2,1)}, u32[]{:S(2)}) copy-start(bf16[128,4096]{1,0:T(8,128)(2,1)} %cot_ref.1) | copy-start | bytes 3145732

commit v2 on v1

--- a/solution.py
+++ b/solution.py
@@ -9,6 +9,8 @@
 
 SEQ_AVG = 8192
 CHUNKS = 8
+STRIP = 16
+LEAD = 1
 
 
 def fisher_columns(arrived, hidden_rows, seq_table, seq_count, window):
@@ -80,12 +82,13 @@
 
 def gather_kernel(
     layers, cap_rows, seq_count, chunks,
-    cot_ref, meta_ref, hidden_ref, out_ref,
+    cot_ref, ids_ref, gate_ref, seq_ref, hidden_ref, out_ref,
     rows_all, meta_all, hidden_buf, hidden_t, pick_w, slot_rows, stage,
-    own_sem, hidden_sem, out_sem, send_sem, recv_sem, meta_send, meta_recv,
+    own_sem, hidden_sem, out_sem, send_sem, recv_sem, strip_send, strip_recv, meta_send, meta_recv,
 ):
     places = 2 * layers
     tok_dev, width = rows_all.shape[3:]
+    main = tok_dev - STRIP
     ffw = hidden_t.shape[0]
     me = lax.axis_index("expert")
     core = lax.rem(me, 2)
@@ -99,10 +102,22 @@
         columns = pl.ds(pl.multiple_of(c * width, width), width)
         return pltpu.make_async_copy(cot_ref.at[:, columns], rows_all.at[c, core, place], own_sem.at[c])
 
-    def rows_copy(c, plane, origin, way):
+    def strip_copy(c, origin, way):
+        strip = rows_all.at[c, core, origin, pl.ds(main, STRIP)]
         return pltpu.make_async_remote_copy(
-            src_ref=rows_all.at[c, plane, origin],
-            dst_ref=rows_all.at[c, plane, origin],
+            src_ref=strip,
+            dst_ref=strip,
+            send_sem=strip_send.at[c, origin // 2, way],
+            recv_sem=strip_recv.at[c, origin // 2],
+            device_id={"expert": device[way]},
+            device_id_type=MESH,
+        )
+
+    def rows_copy(c, plane, origin, way, most=False):
+        piece = rows_all.at[c, plane, origin, pl.ds(0, main)] if most else rows_all.at[c, plane, origin]
+        return pltpu.make_async_remote_copy(
+            src_ref=piece,
+            dst_ref=piece,
             send_sem=send_sem.at[c, origin, way],
             recv_sem=recv_sem.at[c, plane, origin],
             device_id={"expert": device[way]},
@@ -124,27 +139,32 @@
         slot = lax.rem(c, 2)
         return pltpu.make_async_copy(stage.at[slot], out_ref.at[0, :, columns], out_sem.at[slot])
 
-    def send(c, origin, ways):
-        @pl.when(c == 0)
+    def send(c, origin, ways, most=False):
+        @pl.when(jnp.int32(c) == 0)
         def _():
             for way in ways:
                 meta_copy(core, origin, way).start()
 
         for way in ways:
-            rows_copy(c, core, origin, way).start()
-
-    def arrive(c, plane, origin):
+            rows_copy(c, core, origin, way, most).start()
+
+    def arrive(c, plane, origin, most=False):
         @pl.when(c == 0)
         def _():
             meta_copy(plane, origin, SIBLING).wait_recv()
 
-        rows_copy(c, plane, origin, SIBLING).wait_recv()
+        rows_copy(c, plane, origin, SIBLING, most).wait_recv()
 
     hidden_copy = pltpu.make_async_copy(hidden_ref.at[0], hidden_buf, hidden_sem)
     for c in range(chunks):
         own_copy(c).start()
     hidden_copy.start()
-    meta_all[core, place] = meta_ref[...]
+    top = ids_ref.shape[0]
+    meta_all[core, place, 0:top] = ids_ref[...].astype(jnp.float32)
+    meta_all[core, place, top:2 * top] = gate_ref[...].astype(jnp.float32)
+    meta_all[core, place, 2 * top:3 * top] = jnp.broadcast_to(
+        seq_ref[...].astype(jnp.float32), (top, tok_dev)
+    )
 
     barrier = pltpu.get_barrier_semaphore()
     for way in (ACROSS, SIBLING):
@@ -182,13 +202,40 @@
                 def _():
                     send(c, origin, (way,))
 
-                send(c, origin, (ACROSS, SIBLING))
+                send(c, origin, (ACROSS,), True)
+                send(c, origin, (SIBLING,))
+
+    def same_layer(c):
+        origin = z * 2 + 1 - y
+        arrive(c, core, origin)
+        for there, way in ((has_up, UP), (has_down, DOWN)):
+            @pl.when(there)
+            def _():
+                strip_copy(c, origin, way).start()
+
+        send(c, origin, (SIBLING,))
+
+    def relay_strip(c, hop):
+        for source, there, onward, way in (
+            (z - hop, z >= hop, has_up, UP),
+            (z + hop, z + hop < layers, has_down, DOWN),
+        ):
+            @pl.when(there)
+            def _():
+                origin = source * 2 + 1 - y
+                strip_copy(c, origin, way).wait_recv()
+
+                @pl.when(onward)
+                def _():
+                    strip_copy(c, origin, way).start()
 
     def from_across(c):
         for layer in range(layers):
-            origin = layer * 2 + 1 - y
-            arrive(c, core, origin)
-            send(c, origin, (SIBLING,))
+            @pl.when(z != layer)
+            def _():
+                origin = layer * 2 + 1 - y
+                arrive(c, core, origin, True)
+                send(c, origin, (SIBLING,))
 
     def transpose_hidden():
         hidden_copy.wait()
@@ -247,18 +294,18 @@
             out_copy(c - 2).wait()
 
         slot = lax.rem(c, 2)
-        tall = 256
-
-        def squares(m, _):
-            part = pl.ds(pl.multiple_of(m * tall, tall), tall)
+        wide = 256
+
+        def squares(n, _):
+            part = pl.ds(pl.multiple_of(n * wide, wide), wide)
             total = None
             for s in range(seq_count):
-                grad = jnp.dot(hidden_t[part, :], slot_rows[s], preferred_element_type=jnp.float32)
+                grad = jnp.dot(hidden_t[...], slot_rows[s, :, part], preferred_element_type=jnp.float32)
                 total = grad * grad if total is None else total + grad * grad
-            stage[slot, part, :] = total.astype(jnp.bfloat16)
+            stage[slot, :, part] = total.astype(jnp.bfloat16)
             return 0
 
-        lax.fori_loop(0, ffw // tall, squares, 0)
+        lax.fori_loop(0, width // wide, squares, 0)
         out_copy(c).start()
 
     def within(c, act):
@@ -267,7 +314,7 @@
             act(c)
 
     def step(t, _):
-        within(t, start_own)
+        within(t + LEAD, start_own)
 
         @pl.when(t == 1)
         def _():
@@ -275,32 +322,52 @@
 
         for hop in range(layers - 1, 0, -1):
             within(t - hop, lambda c: relay(c, hop))
+        within(t - 1, same_layer)
+        for hop in range(layers - 1, 0, -1):
+            within(t - 1 - hop, lambda c: relay_strip(c, hop))
         within(t - layers, from_across)
-        within(t - layers - 1, finish)
+        within(t - layers, finish)
         return 0
 
-    lax.fori_loop(0, chunks + layers + 1, step, 0)
-
-    def sent_all(c, wait):
+    for c in range(LEAD):
+        start_own(c)
+    lax.fori_loop(0, chunks + layers, step, 0)
+
+    def sent_all(wait, wait_strip):
         for layer in range(layers):
             @pl.when(has_up & (layer <= z))
             def _():
                 wait(layer * 2 + y, UP)
+                wait_strip(layer * 2 + 1 - y, UP)
 
             @pl.when(has_down & (layer >= z))
             def _():
                 wait(layer * 2 + y, DOWN)
-
-            wait(layer * 2 + y, ACROSS)
+                wait_strip(layer * 2 + 1 - y, DOWN)
+
+            @pl.when(z == layer)
+            def _():
+                wait(layer * 2 + y, ACROSS)
+
+            @pl.when(z != layer)
+            def _():
+                wait(layer * 2 + y, ACROSS, True)
+
             wait(layer * 2 + y, SIBLING)
             wait(layer * 2 + 1 - y, SIBLING)
 
     def drain(c, _):
-        sent_all(c, lambda origin, way: rows_copy(c, core, origin, way).wait_send())
+        sent_all(
+            lambda origin, way, most=False: rows_copy(c, core, origin, way, most).wait_send(),
+            lambda origin, way: strip_copy(c, origin, way).wait_send(),
+        )
         return 0
 
     lax.fori_loop(0, chunks, drain, 0)
-    sent_all(0, lambda origin, way: meta_copy(core, origin, way).wait_send())
+    sent_all(
+        lambda origin, way, most=False: meta_copy(core, origin, way).wait_send(),
+        lambda origin, way: None,
+    )
     for c in range(max(chunks - 2, 0), chunks):
         out_copy(c).wait()
 
@@ -315,19 +382,13 @@
     chunks = CHUNKS
     width = depth // chunks
     top = expert_ids.shape[1]
-    meta = jnp.concatenate(
-        [
-            expert_ids.T.astype(jnp.float32),
-            gate_probs.T.astype(jnp.float32),
-            jnp.broadcast_to(seq_ids.astype(jnp.float32)[None, :], (top, tok_dev)),
-        ],
-        axis=0,
-    )
     return pl.pallas_call(
         functools.partial(gather_kernel, layers, cap_rows, seq_count, chunks),
         out_shape=jax.ShapeDtypeStruct((1, ffw, depth), jnp.bfloat16),
         in_specs=[
             pl.BlockSpec(memory_space=pl.ANY),
+            pl.BlockSpec(memory_space=pltpu.VMEM),
+            pl.BlockSpec(memory_space=pltpu.VMEM),
             pl.BlockSpec(memory_space=pltpu.VMEM),
             pl.BlockSpec(memory_space=pl.ANY),
         ],
@@ -345,6 +406,8 @@
             pltpu.SemaphoreType.DMA((2,)),
             pltpu.SemaphoreType.DMA((chunks, 2 * layers, 4)),
             pltpu.SemaphoreType.DMA((chunks, 2, 2 * layers)),
+            pltpu.SemaphoreType.DMA((chunks, layers, 2)),
+            pltpu.SemaphoreType.DMA((chunks, layers)),
             pltpu.SemaphoreType.DMA((2 * layers, 4)),
             pltpu.SemaphoreType.DMA((2, 2 * layers)),
         ],
@@ -354,9 +417,9 @@
             transcendentals=0,
         ),
         compiler_params=pltpu.CompilerParams(
-            collective_id=0, has_side_effects=True, vmem_limit_bytes=52 * 1024 * 1024
+            collective_id=0, has_side_effects=True, vmem_limit_bytes=60 * 1024 * 1024
         ),
-    )(cotangent, meta, hidden_saved)
+    )(cotangent, expert_ids.T, gate_probs.T, seq_ids[None, :], hidden_saved)
 
 
 def parts(cotangent, expert_ids, gate_probs, seq_ids, hidden_saved):

time: 120 us -> 109 us (0.908)
  Pallas kernels: 111 us -> 102 us
  other arithmetic: 2.03 us -> 0 us
  local copies, waits for them, and re-layouts: 7.51 us -> 6.29 us
    pallas_call x1, Pallas kernels: 111 us -> 102 us  [gather_shards(): pl.pallas_call(functools.partial(gather_kernel, layers, cap_rows, seq_cou...]
    convert_element_type x3 -> x0, other arithmetic: 2.03 us -> none  [the longest x1 0.69 us: gather_shards(): expert_ids.T.astype(jnp.float32)]
    unnamed x3 -> x1, local copies, waits for them, and re-layouts: 7.51 us -> 6.29 us
where the time goes in v2:
time: 109 us
  Pallas kernels  102 us (94%)
  local copies, waits for them, and re-layouts  6.29 us (6%)
    pallas_call x1, Pallas kernels, gather_shards(): pl.pallas_call(functools.partial(gather_kernel, layers, cap_rows, seq_cou...  102 us
    unnamed x1, local copies, waits for them, and re-layouts  6.29 us

profile of v2, /device:TPU:0, one launch (start us, length us, event | category | flops | bytes accessed | tf_op | source)
XLA Modules:
  0.0 108.8 jit_solution(12992386833604783663)
XLA Ops:
  0.0 102.5 %shard_map.55 = bf16[1,768,4096]{2,1,0:T(8,128)(2,1)} custom-call(bf16[128,4096]{1,0:T(8,128)(2,1)} %cot_ref.1, s32[8,128]{1,0:T(8,128)} %bitcast.3, bf16[8,128]{1,0:T(8,128)(2,1)} %bitcast.4, s32[1,128]{1,0:T(1,128)} %bitcast.5, bf16[1,1280,768]{2,1,0:T(8,128)(2,1)} %hidden_ref.1), custom_call_target="tpu_custom_call" | custom-call | flops 16106127360 | bytes 9306112 | tf_op jit(solution)/shard_map/pallas_call | solution.py:385
  102.5 6.3 %copy.7 = bf16[1,768,4096]{2,1,0:T(8,128)(2,1)} copy(bf16[1,768,4096]{2,1,0:T(8,128)(2,1)} %shard_map.55) | data formatting | bytes 12582912

commit v3 on v2

--- a/solution.py
+++ b/solution.py
@@ -287,7 +287,7 @@
                     slot_rows[s, pl.ds(first, cap_rows), :] = sent[s * cap_rows:(s + 1) * cap_rows]
             return 0
 
-        lax.fori_loop(0, places, dispatch, 0)
+        lax.fori_loop(0, places, dispatch, 0, unroll=4)
 
         @pl.when(c >= 2)
         def _():
@@ -322,9 +322,8 @@
 
         for hop in range(layers - 1, 0, -1):
             within(t - hop, lambda c: relay(c, hop))
+            within(t - 1 - hop, lambda c: relay_strip(c, hop))
         within(t - 1, same_layer)
-        for hop in range(layers - 1, 0, -1):
-            within(t - 1 - hop, lambda c: relay_strip(c, hop))
         within(t - layers, from_across)
         within(t - layers, finish)
         return 0

time: 109 us -> 107 us (0.982); the launches traced: 109 us -> 105 us
  Pallas kernels: 102 us -> 99.1 us
    pallas_call x1, Pallas kernels: 102 us -> 99.1 us  [gather_shards(): pl.pallas_call(functools.partial(gather_kernel, layers, cap_rows, seq_cou...]
where the time goes in v3:
time: 107 us; the launch traced here: 105 us
  Pallas kernels  99.1 us (93%)
  local copies, waits for them, and re-layouts  6.29 us (6%)
    pallas_call x1, Pallas kernels, gather_shards(): pl.pallas_call(functools.partial(gather_kernel, layers, cap_rows, seq_cou...  99.1 us
    unnamed x1, local copies, waits for them, and re-layouts  6.29 us

profile of v3, /device:TPU:0, one launch (start us, length us, event | category | flops | bytes accessed | tf_op | source)
XLA Modules:
  0.0 105.4 jit_solution(9073243755640234379)
XLA Ops:
  0.0 99.1 %shard_map.55 = bf16[1,768,4096]{2,1,0:T(8,128)(2,1)} custom-call(bf16[128,4096]{1,0:T(8,128)(2,1)} %cot_ref.1, s32[8,128]{1,0:T(8,128)} %bitcast.3, bf16[8,128]{1,0:T(8,128)(2,1)} %bitcast.4, s32[1,128]{1,0:T(1,128)} %bitcast.5, bf16[1,1280,768]{2,1,0:T(8,128)(2,1)} %hidden_ref.1), custom_call_target="tpu_custom_call" | custom-call | flops 16106127360 | bytes 9306112 | tf_op jit(solution)/shard_map/pallas_call | solution.py:384
  99.1 6.3 %copy.7 = bf16[1,768,4096]{2,1,0:T(8,128)(2,1)} copy(bf16[1,768,4096]{2,1,0:T(8,128)(2,1)} %shard_map.55) | data formatting | bytes 12582912
